TPU v7x, 512 devices: a whole 4x8x8 slice. The times are simulated.
512 devices in a mesh: dom: 64 (over y, x, core), feat: 8 (over z).
Axes of the slice: x: 4, y: 8, z: 8, core: 2. Of those that a mesh axis runs over, the one named last changes fastest.
Arguments:
- features: bfloat16 [512, 196608], P('feat', 'dom'), may hold values from -16 to 16
- weights: bfloat16 [2, 512, 512], replicated, may hold values from -0.1875 to 0.1875
- tile_values: bfloat16 [4608, 128, 128], P('dom'), may hold values from 0 to 0.099609375
- tile_blocks: int32 [4608, 2], P('dom'), may hold values from 0 to 31
- tile_counts: int32 [64], P('dom'), may hold values from 36 to 72
- replica: int32 [64, 64, 16], P('dom'), may hold values from -1 to 3071, as said below
- cotangent: bfloat16 [512, 196608], P(None, ('dom', 'feat')), may hold values from -6 to 6
Outputs:
- output: bfloat16 [512, 196608], P(None, ('dom', 'feat'))
- feature_grad: bfloat16 [512, 196608], P('feat', 'dom')
- weight_grad: float32 [2, 512, 512], P(None, 'feat')
Inputs may be any that keep to these rules, and one draw needn't show every extreme that they name: `tile_blocks`: column 0 names a tile's source block and column 1 its destination block. replica[q, p, k] is the master slot on partition q of the vertex in mirror slot q * 16 + k of partition p, or -1 for an unused slot; the used slots of a pair (q, p) come first; no partition mirrors its own masters; each master partition fills all 16 slots toward at least one partition.
All inputs are finite; a program needn't handle non-finite values.
Results may differ from a plain program's by a relative error of at most 0.0058.
Values may be sent and summed in bfloat16 or wider, within the bound.
A program may use at most 64 MiB of HBM per device.

v0:
```python
import jax
import jax.numpy as jnp
from jax import lax
from jax.sharding import PartitionSpec as P


def gathered_total(x, axis):
    pieces = lax.all_gather(x, axis).astype(jnp.float32)
    return pieces.sum(axis=0)


def local(features, weights, tile_values, tile_blocks, tile_counts, replica, cotangent):
    feat_width, masters = features.shape
    tile_size = tile_values.shape[1]
    replica_rows = replica[0]
    slot_used = (replica_rows >= 0).reshape(-1)
    slot_index = jnp.where(replica_rows >= 0, replica_rows, 0).reshape(-1)
    tile_live = (jnp.arange(tile_values.shape[0]) < tile_counts[0]).astype(jnp.float32)
    source_blocks = tile_blocks[:, 0]
    target_blocks = tile_blocks[:, 1]

    def pull_mirrors(values_in):
        outgoing = jnp.where(
            slot_used[None, :],
            jnp.take(values_in, slot_index, axis=1),
            jnp.zeros((), values_in.dtype),
        )
        return lax.all_to_all(outgoing, "dom", split_axis=1, concat_axis=1, tiled=True)

    def push_mirrors(partial_value):
        incoming = lax.all_to_all(
            partial_value[:, masters:].astype(jnp.bfloat16),
            "dom",
            split_axis=1,
            concat_axis=1,
            tiled=True,
        ).astype(jnp.float32)
        targets = jnp.where(slot_used, slot_index, masters)
        return partial_value[:, :masters].at[:, targets].add(incoming, mode="drop")

    def spread(own_cols, forward):
        local_cols = jnp.concatenate([own_cols, pull_mirrors(own_cols)], 1)
        nblocks = local_cols.shape[1] // tile_size
        blocks = local_cols.reshape(feat_width, nblocks, tile_size)
        if forward:
            picked = jnp.take(blocks, source_blocks, axis=1)
            contrib = jnp.einsum(
                "fts,tsd->ftd", picked, tile_values, preferred_element_type=jnp.float32
            )
            segment = target_blocks
        else:
            picked = jnp.take(blocks, target_blocks, axis=1)
            contrib = jnp.einsum(
                "ftd,tsd->fts", picked, tile_values, preferred_element_type=jnp.float32
            )
            segment = source_blocks
        onehot = (segment[:, None] == jnp.arange(nblocks)[None, :]).astype(jnp.float32) * tile_live[
            :, None
        ]
        partial_value = jnp.einsum("ftd,tb->fbd", contrib, onehot, precision=lax.Precision.HIGHEST)
        return push_mirrors(partial_value.reshape(feat_width, nblocks * tile_size))

    aggregate = spread(features, True).astype(jnp.bfloat16)
    feat_rows, agg_rows = (
        lax.all_to_all(features, "feat", split_axis=1, concat_axis=0, tiled=True),
        lax.all_to_all(aggregate, "feat", split_axis=1, concat_axis=0, tiled=True),
    )
    preact = jnp.einsum("io,iv->ov", weights[0], feat_rows, preferred_element_type=jnp.float32)
    preact = preact + jnp.einsum(
        "io,iv->ov", weights[1], agg_rows, preferred_element_type=jnp.float32
    )
    sigmoid_z = jax.nn.sigmoid(preact)
    output = (preact * sigmoid_z).astype(jnp.bfloat16)
    slope = sigmoid_z * (1.0 + preact * (1.0 - sigmoid_z))
    pre_grad = (cotangent.astype(jnp.float32) * slope).astype(jnp.bfloat16)
    slice_start = lax.axis_index("feat") * feat_width
    grad_cols = lax.all_gather(pre_grad, "feat", axis=1, tiled=True)
    weight_slice = lax.dynamic_slice_in_dim(weights, slice_start, feat_width, 1)
    terms = jnp.stack(
        [
            jnp.einsum("iv,ov->io", features, grad_cols, preferred_element_type=jnp.float32),
            jnp.einsum("iv,ov->io", aggregate, grad_cols, preferred_element_type=jnp.float32),
        ]
    )
    weight_grad = gathered_total(terms.astype(jnp.bfloat16), "dom").astype(jnp.float32)
    back_slices = jnp.einsum(
        "kio,ov->kiv", weight_slice, grad_cols, preferred_element_type=jnp.float32
    ).astype(jnp.bfloat16)
    self_grad = back_slices[0]
    agg_grad = back_slices[1]
    back_terms = spread(agg_grad, False)
    feature_grad = (self_grad.astype(jnp.float32) + back_terms).astype(jnp.bfloat16)
    return (output, feature_grad, weight_grad)


def solution(mesh):
    return jax.shard_map(
        local,
        mesh=mesh,
        in_specs=(
            P("feat", "dom"),
            P(),
            P("dom", None, None),
            P("dom", None),
            P("dom"),
            P("dom", None, None),
            P(None, ("dom", "feat")),
        ),
        out_specs=(P(None, ("dom", "feat")), P("feat", "dom"), P(None, "feat", None)),
        check_vma=False,
    )
```

profile of v0, /device:TPU:1, one launch (start us, length us, event | category | flops | bytes accessed | tf_op | source)
XLA Modules:
  0.0 258.0 jit_solution(7112404868492813658)
XLA Ops:
  7.2 0.9 copy.71
  8.8 1.4 copy.72
  10.1 4.3 %gather_fusion = bf16[1024,64]{1,0:T(8,128)(2,1)} fusion(bf16[64,3072]{0,1:T(8,128)(2,1)S(1)} %copy.72, s32[1024]{0:T(1024)S(1)} %fusion.34), kind=kCustom, calls=%fused_computation.clone | custom fusion | bytes 266240 | tf_op jit(solution)/shard_map/jit(_take)/gather | solution.py:25
  14.5 1.3 bitcast_select_fusion.1
  15.8 0.8 reshape.201
  16.6 11.6 %all-to-all-start.1 = ((bf16[64,2,512]{2,1,0:T(2,128)(2,1)}), bf16[64,2,512]{2,1,0:T(2,128)(2,1)S(1)}, u32[]{:S(2)}, u32[]{:S(2)}) async-start(bf16[64,2,512]{2,1,0:T(2,128)(2,1)} %reshape.201), calls=%async_computation.1 | async-start | bytes 262144 | tf_op jit(solution)/shard_map/all_to_all | solution.py:28
  29.5 1.3 slice_bitcast_fusion.2
  30.8 8.6 %all-to-all-done.1 = bf16[64,2,512]{2,1,0:T(2,128)(2,1)S(1)} async-done(((bf16[64,2,512]{2,1,0:T(2,128)(2,1)}), bf16[64,2,512]{2,1,0:T(2,128)(2,1)S(1)}, u32[]{:S(2)}, u32[]{:S(2)}) %all-to-all-start.1) | async-done | bytes 131104 | tf_op jit(solution)/shard_map/all_to_all | solution.py:28
  39.9 1.8 gather_fusion.1
  41.7 2.1 convolution_bitcast_fusion.1
  43.8 2.7 %fusion.3 = f32[32,64,128]{2,0,1:T(8,128)S(1)} fusion(f32[64,72,128]{2,0,1:T(8,128)S(1)} %convolution_bitcast_fusion.1, f32[72]{0:T(128)S(1)} %compare_convert_fusion, s32[72]{0:T(128)S(1)} %get-tuple-element.29), kind=kOutput, calls=%fused_computation.11 | convolution fusion | flops 226497024 | bytes 3408448 | tf_op jit(solution)/shard_map/ftd,tb->fbd/dot_general | solution.py:60
  47.1 1.0 copy-done.3
  48.3 0.8 reshape.203
  49.1 4.4 %all-to-all-start.2 = ((bf16[64,2,512]{2,1,0:T(2,128)(2,1)}), bf16[64,2,512]{2,1,0:T(2,128)(2,1)S(1)}, u32[]{:S(2)}, u32[]{:S(2)}) async-start(bf16[64,2,512]{2,1,0:T(2,128)(2,1)} %reshape.203), calls=%async_computation.2 | async-start | bytes 262144 | tf_op jit(solution)/shard_map/all_to_all | solution.py:31
  54.3 10.6 %all-to-all-done.2 = bf16[64,2,512]{2,1,0:T(2,128)(2,1)S(1)} async-done(((bf16[64,2,512]{2,1,0:T(2,128)(2,1)}), bf16[64,2,512]{2,1,0:T(2,128)(2,1)S(1)}, u32[]{:S(2)}, u32[]{:S(2)}) %all-to-all-start.2) | async-done | bytes 131104 | tf_op jit(solution)/shard_map/all_to_all | solution.py:31
  64.9 10.0 %all-to-all-start = ((bf16[64,8,384]{2,0,1:T(8,128)(2,1)}), bf16[64,8,384]{2,0,1:T(8,128)(2,1)}, u32[]{:S(2)}, u32[]{:S(2)}) async-start(bf16[64,8,384]{2,0,1:T(8,128)(2,1)} %bitcast.122), calls=%async_computation | async-start | bytes 786432 | tf_op jit(solution)/shard_map/all_to_all | solution.py:65
  75.6 1.2 slice.50
  76.8 1.6 copy.78
  78.5 1.1 reshape.204
  79.6 8.2 %scatter_custom_fusion = f32[64,3072]{0,1:T(8,128)} fusion(f32[64,3072]{0,1:T(8,128)} %copy.78, s32[1024]{0:T(1024)} %bitcast.140, bf16[64,1024]{0,1:T(8,128)(2,1)S(1)} %bitcast.133), kind=kCustom, calls=%fused_computation.42 | custom fusion | flops 131072 | bytes 917504 | tf_op jit(solution)/shard_map/scatter-add | solution.py:39
  87.8 1.5 convert_element_type.61
  89.3 1.0 copy.79
  90.3 6.6 %all-to-all-start.3 = ((bf16[64,8,384]{2,0,1:T(8,128)(2,1)}), bf16[64,8,384]{2,0,1:T(8,128)(2,1)}, u32[]{:S(2)}, u32[]{:S(2)}) async-start(bf16[64,8,384]{2,0,1:T(8,128)(2,1)} %copy.79), calls=%async_computation.3 | async-start | bytes 786432 | tf_op jit(solution)/shard_map/all_to_all | solution.py:66
  97.2 2.5 fusion.19
  99.7 10.8 %all-to-all-done.3 = bf16[64,8,384]{2,0,1:T(8,128)(2,1)} async-done(((bf16[64,8,384]{2,0,1:T(8,128)(2,1)}), bf16[64,8,384]{2,0,1:T(8,128)(2,1)}, u32[]{:S(2)}, u32[]{:S(2)}) %all-to-all-start.3) | async-done | bytes 393248 | tf_op jit(solution)/shard_map/all_to_all | solution.py:66
  110.4 3.1 %multiply_convert_fusion = (bf16[512,384]{1,0:T(8,128)(2,1)}, bf16[512,384]{1,0:T(8,128)(2,1)}) fusion(bf16[512,384]{1,0:T(8,128)(2,1)} %param.17, f32[512,384]{1,0:T(8,128)} %fusion.19, bf16[512,384]{1,0:T(8,128)(2,1)} %bitcast.19, bf16[2,512,512]{2,1,0:T(8,128)(2,1)} %param.12), kind=kOutput, calls=%fused_computation.30 | convolution fusion | flops 203882496 | bytes 2883584 | tf_op jit(solution)/shard_map/io,iv->ov/dot_general | solution.py:69
  113.6 38.6 %all-gather.3.cloned.1.call-done = bf16[512,3072]{1,0:T(8,128)(2,1)} async-done(((bf16[512,384]{1,0:T(8,128)(2,1)}), bf16[512,3072]{1,0:T(8,128)(2,1)}) %all-gather.3.cloned.1.call-update) | async-done | bytes 3145744 | tf_op jit(solution)/shard_map/all_gather | solution.py:77
  152.2 3.1 %fusion.13 = bf16[1,1,64,512]{3,2,1,0:T(8,128)(2,1)S(1)} fusion(bf16[64,3072]{0,1:T(8,128)(2,1)S(1)} %convert_element_type.61, bf16[512,3072]{1,0:T(8,128)(2,1)} %all-gather.3.cloned.1.call-done), kind=kOutput, calls=%fused_computation.26 | convolution fusion | flops 201359360 | bytes 3604480 | tf_op jit(solution)/shard_map/iv,ov->io/dot_general | solution.py:82
  155.3 1.1 fusion.12
  157.1 2.6 convolution_convert_fusion
  159.7 0.9 copy-done.4
  161.0 4.3 %gather_fusion.2 = bf16[1024,64]{1,0:T(8,128)(2,1)} fusion(bf16[64,3072]{0,1:T(8,128)(2,1)S(1)} %copy.81, s32[1024]{0:T(1024)S(1)} %fusion.34), kind=kCustom, calls=%fused_computation.2.clone | custom fusion | bytes 266240 | tf_op jit(solution)/shard_map/jit(_take)/gather | solution.py:25
  165.3 1.3 bitcast_select_fusion
  166.8 22.9 %all_to_all.80 = bf16[64,2,512]{2,1,0:T(2,128)(2,1)S(1)} all-to-all(bf16[64,2,512]{2,1,0:T(2,128)(2,1)S(1)} %reshape.205), channel_id=1, replica_groups=mesh['dom'=64,'feat'=8] {'dom'}, dimensions={0} | all-to-all | bytes 262144 | tf_op jit(solution)/shard_map/all_to_all | solution.py:28
  190.2 1.9 gather_fusion.3
  192.1 3.0 %convolution_bitcast_fusion = f32[64,72,128]{2,0,1:T(8,128)S(1)} fusion(bf16[72,128,128]{2,1,0:T(8,128)(2,1)S(1)} %copy-done, bf16[72,64,128]{2,1,0:T(8,128)(2,1)} %gather_fusion.3, pred[72]{0:T(512)(128)(4,1)S(1)} %copy-done.11), kind=kOutput, calls=%fused_computation.13 | convolution fusion | flops 151584768 | bytes 5898312 | tf_op jit(solution)/shard_map/ftd,tsd->fts/dot_general | solution.py:53
  195.1 2.7 %fusion.1 = f32[32,64,128]{2,0,1:T(8,128)S(1)} fusion(f32[64,72,128]{2,0,1:T(8,128)S(1)} %convolution_bitcast_fusion, s32[72]{0:T(128)S(1)} %copy-done.12, f32[72]{0:T(128)S(1)} %copy-done.10), kind=kOutput, calls=%fused_computation.9 | convolution fusion | flops 226497024 | bytes 3408448 | tf_op jit(solution)/shard_map/ftd,tb->fbd/dot_general | solution.py:60
  198.4 0.8 copy.85
  199.3 1.8 reshape.207
  201.0 4.5 %all-to-all-start.5 = ((bf16[64,2,512]{2,1,0:T(2,128)(2,1)}), bf16[64,2,512]{2,1,0:T(2,128)(2,1)S(1)}, u32[]{:S(2)}, u32[]{:S(2)}) async-start(bf16[64,2,512]{2,1,0:T(2,128)(2,1)} %reshape.207), calls=%async_computation.5 | async-start | bytes 262144 | tf_op jit(solution)/shard_map/all_to_all | solution.py:31
  205.5 1.9 slice_add_fusion
  207.5 2.8 %copy.86 = f32[64,3072]{0,1:T(8,128)} copy(f32[64,3072]{1,0:T(8,128)} %slice_add_fusion) | data formatting | bytes 1572864 | tf_op jit(solution)/shard_map/add
  210.3 6.6 %all-to-all-done.5 = bf16[64,2,512]{2,1,0:T(2,128)(2,1)S(1)} async-done(((bf16[64,2,512]{2,1,0:T(2,128)(2,1)}), bf16[64,2,512]{2,1,0:T(2,128)(2,1)S(1)}, u32[]{:S(2)}, u32[]{:S(2)}) %all-to-all-start.5) | async-done | bytes 131104 | tf_op jit(solution)/shard_map/all_to_all | solution.py:31
  217.1 8.2 %scatter_custom_fusion.1 = f32[64,3072]{0,1:T(8,128)} fusion(f32[64,3072]{0,1:T(8,128)} %copy.86, s32[1024]{0:T(1024)} %bitcast.141, bf16[64,1024]{0,1:T(8,128)(2,1)S(1)} %bitcast.132), kind=kCustom, calls=%fused_computation.40 | custom fusion | flops 131072 | bytes 917504 | tf_op jit(solution)/shard_map/scatter-add | solution.py:39
  225.3 1.5 convert_element_type.70
  226.8 1.0 copy.87
  227.8 17.9 %all-gather.5.cloned.1.call-done = bf16[64,2,64,512]{3,2,1,0:T(8,128)(2,1)} async-done(((bf16[1,2,64,512]{3,2,1,0:T(8,128)(2,1)}), bf16[64,2,64,512]{3,2,1,0:T(8,128)(2,1)}) %all-gather.5.cloned.1.call-update) | async-done | bytes 8388624 | tf_op jit(solution)/shard_map/all_gather | solution.py:8
  245.7 5.5 %convert_reduce_fusion = f32[2,64,512]{2,1,0:T(8,128)} fusion(bf16[64,2,64,512]{3,2,1,0:T(8,128)(2,1)} %all-gather.5.cloned.1.call-done), kind=kLoop, calls=%fused_computation.6 | loop fusion | flops 8323072 | bytes 8650752 | tf_op jit(solution)/shard_map/reduce_sum | solution.py:9
  (54 shorter events, 6.8 us)
Async XLA Ops:
  7.2 34.5 %copy-start = (bf16[72,128,128]{2,1,0:T(8,128)(2,1)S(1)}, bf16[72,128,128]{2,1,0:T(8,128)(2,1)}, u32[]{:S(2)}) copy-start(bf16[72,128,128]{2,1,0:T(8,128)(2,1)} %param.13) | copy-start | bytes 7077892
  7.2 32.5 %copy-start.2 = (bf16[64,3072]{1,0:T(8,128)(2,1)S(1)}, bf16[64,3072]{1,0:T(8,128)(2,1)}, u32[]{:S(2)}) copy-start(bf16[64,3072]{1,0:T(8,128)(2,1)} %param.11) | copy-start | bytes 1179652
  7.2 21.0 %copy-start.8 = (s32[72,2]{0,1:T(2,128)S(1)}, s32[72,2]{0,1:T(2,128)}, u32[]{:S(2)}) copy-start(s32[72,2]{0,1:T(2,128)} %param.14) | copy-start | bytes 1732
  8.1 0.6 copy-start.6
  16.6 22.7 %all-to-all-start.1 = ((bf16[64,2,512]{2,1,0:T(2,128)(2,1)}), bf16[64,2,512]{2,1,0:T(2,128)(2,1)S(1)}, u32[]{:S(2)}, u32[]{:S(2)}) async-start(bf16[64,2,512]{2,1,0:T(2,128)(2,1)} %reshape.201), calls=%async_computation.1 | async-start | bytes 262144 | tf_op jit(solution)/shard_map/all_to_all | solution.py:28
  29.5 14.3 %copy-start.9 = (f32[72]{0:T(128)}, f32[72]{0:T(128)S(1)}, u32[]{:S(2)}) copy-start(f32[72]{0:T(128)S(1)} %compare_convert_fusion) | copy-start | bytes 868
  46.4 28.5 %copy-start.7 = (s32[1,64,16]{2,1,0:T(8,128)S(1)}, s32[1,64,16]{2,1,0:T(8,128)}, u32[]{:S(2)}) copy-start(s32[1,64,16]{2,1,0:T(8,128)} %copy-done.6) | copy-start | bytes 12292
  47.1 1.0 copy-start.3
  49.1 15.8 %all-to-all-start.2 = ((bf16[64,2,512]{2,1,0:T(2,128)(2,1)}), bf16[64,2,512]{2,1,0:T(2,128)(2,1)S(1)}, u32[]{:S(2)}, u32[]{:S(2)}) async-start(bf16[64,2,512]{2,1,0:T(2,128)(2,1)} %reshape.203), calls=%async_computation.2 | async-start | bytes 262144 | tf_op jit(solution)/shard_map/all_to_all | solution.py:31
  64.9 10.1 %copy-start.5 = (bf16[64,2,512]{2,1,0:T(2,128)(2,1)}, bf16[64,2,512]{2,1,0:T(2,128)(2,1)S(1)}, u32[]{:S(2)}) copy-start(bf16[64,2,512]{2,1,0:T(2,128)(2,1)S(1)} %all-to-all-done.2) | copy-start | bytes 393220
  64.9 25.4 %all-to-all-start = ((bf16[64,8,384]{2,0,1:T(8,128)(2,1)}), bf16[64,8,384]{2,0,1:T(8,128)(2,1)}, u32[]{:S(2)}, u32[]{:S(2)}) async-start(bf16[64,8,384]{2,0,1:T(8,128)(2,1)} %bitcast.122), calls=%async_computation | async-start | bytes 786432 | tf_op jit(solution)/shard_map/all_to_all | solution.py:65
  90.3 20.1 %all-to-all-start.3 = ((bf16[64,8,384]{2,0,1:T(8,128)(2,1)}), bf16[64,8,384]{2,0,1:T(8,128)(2,1)}, u32[]{:S(2)}, u32[]{:S(2)}) async-start(bf16[64,8,384]{2,0,1:T(8,128)(2,1)} %copy.79), calls=%async_computation.3 | async-start | bytes 786432 | tf_op jit(solution)/shard_map/all_to_all | solution.py:66
  96.9 55.3 %all-gather.3.cloned.1.call-start = ((), (), s32[]{:S(2)}) async-start(), calls=%async_computation.6 | async-start | bytes 3538944 | tf_op jit(solution)/shard_map/all_gather | solution.py:77
  113.6 132.1 %all-gather.5.cloned.1.call-start = ((), (), s32[]{:S(2)}) async-start(), calls=%async_computation.7 | async-start | bytes 8519680 | tf_op jit(solution)/shard_map/all_gather | solution.py:8
  152.2 3.1 %copy-start.1 = (bf16[512,3072]{1,0:T(8,128)(2,1)S(1)}, bf16[512,3072]{1,0:T(8,128)(2,1)}, u32[]{:S(2)}) copy-start(bf16[512,3072]{1,0:T(8,128)(2,1)} %all-gather.3.cloned.1.call-done) | copy-start | bytes 9437188
  159.6 0.9 copy-start.4
  166.6 25.5 %copy-start.11 = (pred[72]{0:T(512)(128)(4,1)S(1)}, pred[72]{0:T(512)(128)(4,1)}, u32[]{:S(2)}) copy-start(pred[72]{0:T(512)(128)(4,1)} %get-tuple-element.20) | copy-start | bytes 220
  192.1 3.0 %copy-start.10 = (f32[72]{0:T(128)S(1)}, f32[72]{0:T(128)}, u32[]{:S(2)}) copy-start(f32[72]{0:T(128)} %copy-done.9) | copy-start | bytes 868
  192.1 3.0 %copy-start.12 = (s32[72]{0:T(128)S(1)}, s32[72]{0:T(128)}, u32[]{:S(2)}) copy-start(s32[72]{0:T(128)} %get-tuple-element.28) | copy-start | bytes 868
  201.0 15.8 %all-to-all-start.5 = ((bf16[64,2,512]{2,1,0:T(2,128)(2,1)}), bf16[64,2,512]{2,1,0:T(2,128)(2,1)S(1)}, u32[]{:S(2)}, u32[]{:S(2)}) async-start(bf16[64,2,512]{2,1,0:T(2,128)(2,1)} %reshape.207), calls=%async_computation.5 | async-start | bytes 262144 | tf_op jit(solution)/shard_map/all_to_all | solution.py:31
Sparse Core Ops, SparseCore 0:
  113.7 38.4 all-gather.2
  157.2 88.4 all-gather.4
where the time goes:
time: 259 us; the launch traced here: 258 us
  waiting for transfers between devices  92.9 us (36%)
  starting transfers between devices  37.5 us (14%)
  local copies, waits for them, and re-layouts  35.4 us (14%)
  other arithmetic  31.5 us (12%)
  blocking collectives  22.9 us (9%)
  matrix products  22.7 us (9%)
  between operations  15 us (6%)
    all_gather x1, waiting for transfers between devices, local(): grad_cols = lax.all_gather(pre_grad, 'feat', axis=1, tiled=True)  38.6 us
    all_to_all x1, blocking collectives, pull_mirrors(): lax.all_to_all(outgoing, 'dom', split_axis=1, concat_axis=1, tiled=True)  22.9 us
    all_gather x1, waiting for transfers between devices, gathered_total(): pieces = lax.all_gather(x, axis).astype(jnp.float32)  17.9 us
    all_to_all x2, waiting for transfers between devices, push_mirrors(): lax.all_to_all(partial_value[:, masters:].astype(jnp.bfloat16), 'dom', sp...  17.1 us
    scatter-add x2, other arithmetic, push_mirrors(): return partial_value[:, :masters].at[:, targets].add(incoming, mode='drop')  16.4 us
    unnamed x39, local copies, waits for them, and re-layouts  12.5 us
    all_to_all x1, starting transfers between devices, pull_mirrors(): lax.all_to_all(outgoing, 'dom', split_axis=1, concat_axis=1, tiled=True)  11.6 us
    all_to_all x1, waiting for transfers between devices, local(): lax.all_to_all(aggregate, 'feat', split_axis=1, concat_axis=0, tiled=True)  10.8 us
  transfers between devices with their start and end apart: 7, of which 6 were waited for; matrix products, arithmetic and copies ran while one was open for 22% of the time, Pallas kernels for 0%

commit v1 on v0

--- a/solution.py
+++ b/solution.py
@@ -74,7 +74,10 @@
     slope = sigmoid_z * (1.0 + preact * (1.0 - sigmoid_z))
     pre_grad = (cotangent.astype(jnp.float32) * slope).astype(jnp.bfloat16)
     slice_start = lax.axis_index("feat") * feat_width
-    grad_cols = lax.all_gather(pre_grad, "feat", axis=1, tiled=True)
+    size = lax.axis_size("feat")
+    tiles = jnp.stack([pre_grad for _ in range(size)])
+    tiles = lax.all_to_all(tiles, "feat", split_axis=0, concat_axis=0)
+    grad_cols = jnp.concatenate(tiles, axis=1)
     weight_slice = lax.dynamic_slice_in_dim(weights, slice_start, feat_width, 1)
     terms = jnp.stack(
         [

time: 259 us -> 289 us (1.12)
  blocking collectives: 22.9 us -> 91.5 us
  waiting for transfers between devices: 92.9 us -> 42.8 us
  local copies, waits for them, and re-layouts: 35.4 us -> 48.7 us
    all_to_all x0 -> x1, blocking collectives: none -> 73.1 us  [local(): tiles = lax.all_to_all(tiles, 'feat', split_axis=0, concat_axis=0)]
    all_gather x1 -> x0, waiting for transfers between devices: 38.6 us -> none  [local(): grad_cols = lax.all_gather(pre_grad, 'feat', axis=1, tiled=True)]
    all_gather x1, waiting for transfers between devices: 17.9 us -> 5.5 us  [gathered_total(): pieces = lax.all_gather(x, axis).astype(jnp.float32)]
    reshape x0 -> x3, local copies, waits for them, and re-layouts: none -> 11.9 us  [local(): grad_cols = jnp.concatenate(tiles, axis=1)]
    all_to_all x1, blocking collectives: 22.9 us -> 18.4 us  [pull_mirrors(): lax.all_to_all(outgoing, 'dom', split_axis=1, concat_axis=1, tiled=True)]
  transfers between devices with their start and end apart: 7 -> 6, of which waited for: 6 -> 5; matrix products, arithmetic and copies ran while one was open for 22% -> 23% of each run, Pallas kernels for 0% -> 0%
where the time goes in v1:
time: 289 us; the launch traced here: 288 us
  blocking collectives  91.5 us (32%)
  local copies, waits for them, and re-layouts  48.7 us (17%)
  waiting for transfers between devices  42.8 us (15%)
  starting transfers between devices  37.4 us (13%)
  other arithmetic  31.5 us (11%)
  matrix products  20.6 us (7%)
  between operations  15 us (5%)
    all_to_all x1, blocking collectives, local(): tiles = lax.all_to_all(tiles, 'feat', split_axis=0, concat_axis=0)  73.1 us
    all_to_all x1, blocking collectives, pull_mirrors(): lax.all_to_all(outgoing, 'dom', split_axis=1, concat_axis=1, tiled=True)  18.4 us
    all_to_all x2, waiting for transfers between devices, push_mirrors(): lax.all_to_all(partial_value[:, masters:].astype(jnp.bfloat16), 'dom', sp...  18 us
    scatter-add x2, other arithmetic, push_mirrors(): return partial_value[:, :masters].at[:, targets].add(incoming, mode='drop')  16.4 us
    unnamed x39, local copies, waits for them, and re-layouts  13.5 us
    reshape x3, local copies, waits for them, and re-layouts, local(): grad_cols = jnp.concatenate(tiles, axis=1)  11.9 us
    all_to_all x1, starting transfers between devices, pull_mirrors(): lax.all_to_all(outgoing, 'dom', split_axis=1, concat_axis=1, tiled=True)  11.6 us
    all_to_all x1, waiting for transfers between devices, local(): lax.all_to_all(aggregate, 'feat', split_axis=1, concat_axis=0, tiled=True)  10.7 us
  transfers between devices with their start and end apart: 6, of which 5 were waited for; matrix products, arithmetic and copies ran while one was open for 23% of the time, Pallas kernels for 0%

profile of v1, /device:TPU:1, one launch (start us, length us, event | category | flops | bytes accessed | tf_op | source)
XLA Modules:
  0.0 287.5 jit_solution(14868256337455290238)
XLA Ops:
  7.2 0.9 copy.72
  8.8 1.4 copy.73
  10.1 4.3 %gather_fusion = bf16[1024,64]{1,0:T(8,128)(2,1)} fusion(bf16[64,3072]{0,1:T(8,128)(2,1)S(1)} %copy.73, s32[1024]{0:T(1024)S(1)} %fusion.33), kind=kCustom, calls=%fused_computation.clone | custom fusion | bytes 266240 | tf_op jit(solution)/shard_map/jit(_take)/gather | solution.py:25
  14.5 1.3 bitcast_select_fusion.1
  16.6 11.6 %all-to-all-start.1 = ((bf16[64,2,512]{2,1,0:T(2,128)(2,1)}), bf16[64,2,512]{2,1,0:T(2,128)(2,1)S(1)}, u32[]{:S(2)}, u32[]{:S(2)}) async-start(bf16[64,2,512]{2,1,0:T(2,128)(2,1)} %reshape.212), calls=%async_computation.1 | async-start | bytes 262144 | tf_op jit(solution)/shard_map/all_to_all | solution.py:28
  29.5 1.3 slice_bitcast_fusion.2
  30.8 8.5 %all-to-all-done.1 = bf16[64,2,512]{2,1,0:T(2,128)(2,1)S(1)} async-done(((bf16[64,2,512]{2,1,0:T(2,128)(2,1)}), bf16[64,2,512]{2,1,0:T(2,128)(2,1)S(1)}, u32[]{:S(2)}, u32[]{:S(2)}) %all-to-all-start.1) | async-done | bytes 131104 | tf_op jit(solution)/shard_map/all_to_all | solution.py:28
  39.9 1.8 gather_fusion.1
  41.7 2.1 convolution_bitcast_fusion.1
  43.8 2.7 fusion.2
  47.1 1.0 copy-done.3
  49.1 4.4 %all-to-all-start.2 = ((bf16[64,2,512]{2,1,0:T(2,128)(2,1)}), bf16[64,2,512]{2,1,0:T(2,128)(2,1)S(1)}, u32[]{:S(2)}, u32[]{:S(2)}) async-start(bf16[64,2,512]{2,1,0:T(2,128)(2,1)} %reshape.214), calls=%async_computation.2 | async-start | bytes 262144 | tf_op jit(solution)/shard_map/all_to_all | solution.py:31
  54.3 10.6 %all-to-all-done.2 = bf16[64,2,512]{2,1,0:T(2,128)(2,1)S(1)} async-done(((bf16[64,2,512]{2,1,0:T(2,128)(2,1)}), bf16[64,2,512]{2,1,0:T(2,128)(2,1)S(1)}, u32[]{:S(2)}, u32[]{:S(2)}) %all-to-all-start.2) | async-done | bytes 131104 | tf_op jit(solution)/shard_map/all_to_all | solution.py:31
  64.9 10.0 %all-to-all-start = ((bf16[64,8,384]{2,0,1:T(8,128)(2,1)}), bf16[64,8,384]{2,0,1:T(8,128)(2,1)}, u32[]{:S(2)}, u32[]{:S(2)}) async-start(bf16[64,8,384]{2,0,1:T(8,128)(2,1)} %bitcast.123), calls=%async_computation | async-start | bytes 786432 | tf_op jit(solution)/shard_map/all_to_all | solution.py:65
  75.6 1.2 slice.50
  76.8 1.6 copy.79
  78.5 1.1 reshape.215
  79.6 8.2 %scatter_custom_fusion = f32[64,3072]{0,1:T(8,128)} fusion(f32[64,3072]{0,1:T(8,128)} %copy.79, s32[1024]{0:T(1024)} %bitcast.145, bf16[64,1024]{0,1:T(8,128)(2,1)S(1)} %bitcast.138), kind=kCustom, calls=%fused_computation.41 | custom fusion | flops 131072 | bytes 917504 | tf_op jit(solution)/shard_map/scatter-add | solution.py:39
  87.8 1.5 convert_element_type.61
  89.2 1.0 copy.80
  90.3 6.6 %all-to-all-start.3 = ((bf16[64,8,384]{2,0,1:T(8,128)(2,1)}), bf16[64,8,384]{2,0,1:T(8,128)(2,1)}, u32[]{:S(2)}, u32[]{:S(2)}) async-start(bf16[64,8,384]{2,0,1:T(8,128)(2,1)} %copy.80), calls=%async_computation.3 | async-start | bytes 786432 | tf_op jit(solution)/shard_map/all_to_all | solution.py:66
  97.1 2.5 fusion.18
  99.6 10.7 %all-to-all-done.3 = bf16[64,8,384]{2,0,1:T(8,128)(2,1)} async-done(((bf16[64,8,384]{2,0,1:T(8,128)(2,1)}), bf16[64,8,384]{2,0,1:T(8,128)(2,1)}, u32[]{:S(2)}, u32[]{:S(2)}) %all-to-all-start.3) | async-done | bytes 393248 | tf_op jit(solution)/shard_map/all_to_all | solution.py:66
  110.4 3.0 %multiply_convert_fusion = (bf16[512,384]{1,0:T(8,128)(2,1)S(1)}, bf16[512,384]{1,0:T(8,128)(2,1)}) fusion(bf16[512,384]{1,0:T(8,128)(2,1)} %param.17, f32[512,384]{1,0:T(8,128)} %fusion.18, bf16[512,384]{1,0:T(8,128)(2,1)} %bitcast.19, bf16[2,512,512]{2,1,0:T(8,128)(2,1)} %param.12), kind=kOutput, calls=%fused_computation.29 | convolution fusion | flops 203882496 | bytes 2883584 | tf_op jit(solution)/shard_map/io,iv->ov/dot_general | solution.py:69
  113.7 73.1 %all_to_all.85 = bf16[8,512,384]{2,1,0:T(8,128)(2,1)S(1)} all-to-all(bf16[8,512,384]{2,1,0:T(8,128)(2,1)S(1)} %stack.8), channel_id=1, replica_groups=mesh['dom'=64,'feat'=8] {'feat'}, dimensions={0} | all-to-all | bytes 6291456 | tf_op jit(solution)/shard_map/all_to_all | solution.py:79
  187.4 1.1 copy-done.1
  188.5 1.1 fusion.12
  189.6 1.1 fusion.11
  191.3 5.5 %copy.82 = bf16[512,8,384]{2,1,0:T(8,128)(2,1)} copy(bf16[512,8,384]{2,0,1:T(8,128)(2,1)} %bitcast.126) | data formatting | bytes 6291456 | tf_op jit(solution)/shard_map/reshape | solution.py:80
  196.8 5.8 %reshape.205 = bf16[512,3072,1]{1,0,2:T(8,128)(2,1)} reshape(bf16[512,8,384]{2,1,0:T(8,128)(2,1)} %copy.82) | data formatting | bytes 6291456 | tf_op jit(solution)/shard_map/reshape | solution.py:80
  202.7 2.5 convolution_convert_fusion
  205.2 0.9 copy-done.4
  206.5 4.3 %gather_fusion.2 = bf16[1024,64]{1,0:T(8,128)(2,1)} fusion(bf16[64,3072]{0,1:T(8,128)(2,1)S(1)} %copy.83, s32[1024]{0:T(1024)S(1)} %fusion.33), kind=kCustom, calls=%fused_computation.2.clone | custom fusion | bytes 266240 | tf_op jit(solution)/shard_map/jit(_take)/gather | solution.py:25
  210.8 1.3 bitcast_select_fusion
  212.3 18.4 %all_to_all.86 = bf16[64,2,512]{2,1,0:T(2,128)(2,1)S(1)} all-to-all(bf16[64,2,512]{2,1,0:T(2,128)(2,1)S(1)} %reshape.216), channel_id=1, replica_groups=mesh['dom'=64,'feat'=8] {'dom'}, dimensions={0} | all-to-all | bytes 262144 | tf_op jit(solution)/shard_map/all_to_all | solution.py:28
  231.2 1.9 gather_fusion.3
  233.1 3.0 %convolution_bitcast_fusion = f32[64,72,128]{2,0,1:T(8,128)S(1)} fusion(bf16[72,128,128]{2,1,0:T(8,128)(2,1)S(1)} %copy-done, bf16[72,64,128]{2,1,0:T(8,128)(2,1)} %gather_fusion.3, pred[72]{0:T(512)(128)(4,1)S(1)} %copy-done.11), kind=kOutput, calls=%fused_computation.12 | convolution fusion | flops 151584768 | bytes 5898312 | tf_op jit(solution)/shard_map/ftd,tsd->fts/dot_general | solution.py:53
  236.1 2.7 fusion
  240.3 1.8 reshape.218
  242.0 4.4 %all-to-all-start.6 = ((bf16[64,2,512]{2,1,0:T(2,128)(2,1)}), bf16[64,2,512]{2,1,0:T(2,128)(2,1)S(1)}, u32[]{:S(2)}, u32[]{:S(2)}) async-start(bf16[64,2,512]{2,1,0:T(2,128)(2,1)} %reshape.218), calls=%async_computation.6 | async-start | bytes 262144 | tf_op jit(solution)/shard_map/all_to_all | solution.py:31
  246.5 2.0 slice_add_fusion
  248.5 2.8 copy.88
  251.3 7.4 %all-to-all-done.6 = bf16[64,2,512]{2,1,0:T(2,128)(2,1)S(1)} async-done(((bf16[64,2,512]{2,1,0:T(2,128)(2,1)}), bf16[64,2,512]{2,1,0:T(2,128)(2,1)S(1)}, u32[]{:S(2)}, u32[]{:S(2)}) %all-to-all-start.6) | async-done | bytes 131104 | tf_op jit(solution)/shard_map/all_to_all | solution.py:31
  258.9 8.2 %scatter_custom_fusion.1 = f32[64,3072]{0,1:T(8,128)} fusion(f32[64,3072]{0,1:T(8,128)} %copy.88, s32[1024]{0:T(1024)} %bitcast.146, bf16[64,1024]{0,1:T(8,128)(2,1)S(1)} %bitcast.137), kind=kCustom, calls=%fused_computation.39 | custom fusion | flops 131072 | bytes 917504 | tf_op jit(solution)/shard_map/scatter-add | solution.py:39
  267.1 1.5 convert_element_type.70
  268.7 1.0 copy.89
  269.7 5.5 %all-gather.2.cloned.1.call-done = bf16[64,2,64,512]{3,2,1,0:T(8,128)(2,1)} async-done(((bf16[1,2,64,512]{3,2,1,0:T(8,128)(2,1)}), bf16[64,2,64,512]{3,2,1,0:T(8,128)(2,1)}) %all-gather.2.cloned.1.call-update) | async-done | bytes 8388624 | tf_op jit(solution)/shard_map/all_gather | solution.py:8
  275.2 5.5 %convert_reduce_fusion = f32[2,64,512]{2,1,0:T(8,128)} fusion(bf16[64,2,64,512]{3,2,1,0:T(8,128)(2,1)} %all-gather.2.cloned.1.call-done), kind=kLoop, calls=%fused_computation.6 | loop fusion | flops 8323072 | bytes 8650752 | tf_op jit(solution)/shard_map/reduce_sum | solution.py:9
  (56 shorter events, 10.2 us)
Async XLA Ops:
  7.2 34.5 %copy-start = (bf16[72,128,128]{2,1,0:T(8,128)(2,1)S(1)}, bf16[72,128,128]{2,1,0:T(8,128)(2,1)}, u32[]{:S(2)}) copy-start(bf16[72,128,128]{2,1,0:T(8,128)(2,1)} %param.13) | copy-start | bytes 7077892
  7.2 32.5 %copy-start.2 = (bf16[64,3072]{1,0:T(8,128)(2,1)S(1)}, bf16[64,3072]{1,0:T(8,128)(2,1)}, u32[]{:S(2)}) copy-start(bf16[64,3072]{1,0:T(8,128)(2,1)} %param.11) | copy-start | bytes 1179652
  7.2 21.0 %copy-start.8 = (s32[72,2]{0,1:T(2,128)S(1)}, s32[72,2]{0,1:T(2,128)}, u32[]{:S(2)}) copy-start(s32[72,2]{0,1:T(2,128)} %param.14) | copy-start | bytes 1732
  8.1 0.6 copy-start.6
  16.6 22.7 %all-to-all-start.1 = ((bf16[64,2,512]{2,1,0:T(2,128)(2,1)}), bf16[64,2,512]{2,1,0:T(2,128)(2,1)S(1)}, u32[]{:S(2)}, u32[]{:S(2)}) async-start(bf16[64,2,512]{2,1,0:T(2,128)(2,1)} %reshape.212), calls=%async_computation.1 | async-start | bytes 262144 | tf_op jit(solution)/shard_map/all_to_all | solution.py:28
  29.5 14.3 %copy-start.9 = (f32[72]{0:T(128)}, f32[72]{0:T(128)S(1)}, u32[]{:S(2)}) copy-start(f32[72]{0:T(128)S(1)} %compare_convert_fusion) | copy-start | bytes 868
  46.4 28.5 %copy-start.7 = (s32[1,64,16]{2,1,0:T(8,128)S(1)}, s32[1,64,16]{2,1,0:T(8,128)}, u32[]{:S(2)}) copy-start(s32[1,64,16]{2,1,0:T(8,128)} %copy-done.6) | copy-start | bytes 12292
  47.0 1.0 copy-start.3
  49.1 15.8 %all-to-all-start.2 = ((bf16[64,2,512]{2,1,0:T(2,128)(2,1)}), bf16[64,2,512]{2,1,0:T(2,128)(2,1)S(1)}, u32[]{:S(2)}, u32[]{:S(2)}) async-start(bf16[64,2,512]{2,1,0:T(2,128)(2,1)} %reshape.214), calls=%async_computation.2 | async-start | bytes 262144 | tf_op jit(solution)/shard_map/all_to_all | solution.py:31
  64.9 10.1 %copy-start.5 = (bf16[64,2,512]{2,1,0:T(2,128)(2,1)}, bf16[64,2,512]{2,1,0:T(2,128)(2,1)S(1)}, u32[]{:S(2)}) copy-start(bf16[64,2,512]{2,1,0:T(2,128)(2,1)S(1)} %all-to-all-done.2) | copy-start | bytes 393220
  64.9 25.4 %all-to-all-start = ((bf16[64,8,384]{2,0,1:T(8,128)(2,1)}), bf16[64,8,384]{2,0,1:T(8,128)(2,1)}, u32[]{:S(2)}, u32[]{:S(2)}) async-start(bf16[64,8,384]{2,0,1:T(8,128)(2,1)} %bitcast.123), calls=%async_computation | async-start | bytes 786432 | tf_op jit(solution)/shard_map/all_to_all | solution.py:65
  90.3 20.1 %all-to-all-start.3 = ((bf16[64,8,384]{2,0,1:T(8,128)(2,1)}), bf16[64,8,384]{2,0,1:T(8,128)(2,1)}, u32[]{:S(2)}, u32[]{:S(2)}) async-start(bf16[64,8,384]{2,0,1:T(8,128)(2,1)} %copy.80), calls=%async_computation.3 | async-start | bytes 786432 | tf_op jit(solution)/shard_map/all_to_all | solution.py:66
  96.9 178.3 %all-gather.2.cloned.1.call-start = ((), (), s32[]{:S(2)}) async-start(), calls=%async_computation.7 | async-start | bytes 8519680 | tf_op jit(solution)/shard_map/all_gather | solution.py:8
  186.8 1.7 copy-start.1
  205.2 0.9 copy-start.4
  212.1 21.0 %copy-start.11 = (pred[72]{0:T(512)(128)(4,1)S(1)}, pred[72]{0:T(512)(128)(4,1)}, u32[]{:S(2)}) copy-start(pred[72]{0:T(512)(128)(4,1)} %get-tuple-element.20) | copy-start | bytes 220
  233.1 3.0 %copy-start.10 = (f32[72]{0:T(128)S(1)}, f32[72]{0:T(128)}, u32[]{:S(2)}) copy-start(f32[72]{0:T(128)} %copy-done.9) | copy-start | bytes 868
  233.1 3.0 %copy-start.12 = (s32[72]{0:T(128)S(1)}, s32[72]{0:T(128)}, u32[]{:S(2)}) copy-start(s32[72]{0:T(128)} %get-tuple-element.28) | copy-start | bytes 868
  242.0 16.7 %all-to-all-start.6 = ((bf16[64,2,512]{2,1,0:T(2,128)(2,1)}), bf16[64,2,512]{2,1,0:T(2,128)(2,1)S(1)}, u32[]{:S(2)}, u32[]{:S(2)}) async-start(bf16[64,2,512]{2,1,0:T(2,128)(2,1)} %reshape.218), calls=%async_computation.6 | async-start | bytes 262144 | tf_op jit(solution)/shard_map/all_to_all | solution.py:31
Sparse Core Ops, SparseCore 0:
  191.5 83.6 all-gather.1
